TPU v7x, 512 devices: a whole 4x4x16 slice. The times are simulated.
512 devices in a mesh: row: 16 (over z_lo, core), col: 32 (over x, y, z_hi).
Axes of the slice: x: 4, y: 4, z: 16 (z_hi: 2, z_lo: 8; z = z_hi * 8 + z_lo), core: 2. Of those that a mesh axis runs over, the one named last changes fastest.
Arguments:
- greens: float32 [13824, 13824], P('row', 'col')
- accepted_sites: int32 [256], replicated, may hold values from 0 to 13823, as said below
- field_values: int32 [256], replicated, may hold values from -1 to 1, as said below
- left_a: float32 [96, 144, 144], P('row')
- left_b: float32 [96, 144, 144], P('row')
- right_a: float32 [96, 144, 144], P('col')
- right_b: float32 [96, 144, 144], P('col')
Outputs:
- wrapped: float32 [13824, 13824], P('row', 'col')
Inputs may be any that keep to these rules, and one draw needn't show every extreme that they name: `accepted_sites`: site k (from 0) lies in [k * 54, (k + 1) * 54), so the sites rise. `field_values`: each value is -1 or 1.
All inputs are finite; a program needn't handle non-finite values.
Results may differ from a plain program's by a relative error of at most 0.000073.
Values sent between devices are 32-bit elements; how exact they have to be, the bound alone decides.
A program may use at most 64 MiB of HBM per device.

v0:
```python
import jax
import jax.numpy as jnp
from jax import lax
from jax.sharding import PartitionSpec as P

highest = lax.Precision.HIGHEST
coupling = 0.45


def padded_2(x, sides, width):
    for axis, dim in sides:
        size, length = (lax.axis_size(axis), x.shape[dim])
        up = [(i, (i + 1) % size) for i in range(size)]
        down = [(j, i) for i, j in up]
        last = lax.slice_in_dim(x, length - width, length, axis=dim)
        leading = lax.slice_in_dim(x, 0, width, axis=dim)
        before = lax.ppermute(last, axis, up)
        after = lax.ppermute(leading, axis, down)
        x = jnp.concatenate([before, x, after], axis=dim)
    return x


def from_behind(value, axis, steps):
    count = lax.axis_size(axis)
    pairs = [(source, (source + steps) % count) for source in range(count)]
    return lax.ppermute(value, axis, pairs)


def blocks_left(blocks, matrix):
    number = blocks.shape[0]
    cluster = blocks.shape[1]
    product = jnp.einsum(
        "cab,cbm->cam", blocks, matrix.reshape(number, cluster, matrix.shape[1]), precision=highest
    )
    return product.reshape(number * cluster, matrix.shape[1])


def blocks_right(matrix, blocks):
    number = blocks.shape[0]
    cluster = blocks.shape[1]
    product = jnp.einsum(
        "mcb,cba->mca", matrix.reshape(matrix.shape[0], number, cluster), blocks, precision=highest
    )
    return product.reshape(matrix.shape[0], number * cluster)


def left_apply(matrix, first_blocks, second_blocks, carried):
    height = matrix.shape[0]
    margin = first_blocks.shape[1] // 2
    inner = blocks_left(first_blocks, matrix)
    padded = padded_2(inner, (("row", 0),), margin)
    stacked = jnp.concatenate([carried[None], second_blocks], axis=0)
    return blocks_left(stacked, padded)[margin : margin + height]


def right_apply(matrix, first_blocks, second_blocks, carried):
    breadth = matrix.shape[1]
    margin = first_blocks.shape[1] // 2
    inner = blocks_right(matrix, first_blocks)
    padded = padded_2(inner, (("col", 1),), margin)
    stacked = jnp.concatenate([carried[None], second_blocks], axis=0)
    return blocks_right(padded, stacked)[:, margin : margin + breadth]


def whole_apply(matrix, left_a, left_b, right_a, right_b, carried_left, carried_right):
    left_done = left_apply(matrix, left_a, left_b, carried_left)
    return right_apply(left_done, right_a, right_b, carried_right)


def on_device(greens, accepted_sites, field_values, left_a, left_b, right_a, right_b):
    height = greens.shape[0]
    breadth = greens.shape[1]
    accepted = accepted_sites.shape[0]
    row_base = lax.axis_index("row") * height
    col_base = lax.axis_index("col") * breadth
    col_hit = (
        accepted_sites[None, :]
        == col_base + lax.broadcasted_iota(jnp.int32, (breadth, accepted), 0)
    ).astype(jnp.float32)
    row_hit = (
        accepted_sites[:, None] == row_base + lax.broadcasted_iota(jnp.int32, (accepted, height), 1)
    ).astype(jnp.float32)
    g_cols = lax.psum(jnp.dot(greens, col_hit, precision=highest), "col")
    g_rows = lax.psum(jnp.dot(row_hit, greens, precision=highest), "row")
    g_pair = lax.psum(jnp.dot(g_rows, col_hit, precision=highest), "col")
    shifts = jnp.exp(-2.0 * coupling * field_values.astype(jnp.float32)) - 1.0
    identity = jnp.eye(accepted, dtype=jnp.float32)
    capacity = identity + (identity - g_pair) * shifts[None, :]
    normal_matrix = jnp.dot(capacity.T, capacity, precision=highest)
    lower_factor = jnp.linalg.cholesky(normal_matrix)
    middle = lax.linalg.triangular_solve(lower_factor, capacity.T, left_side=True, lower=True)
    inverse = lax.linalg.triangular_solve(
        lower_factor, middle, left_side=True, lower=True, transpose_a=True
    )
    scaled = shifts[:, None] * inverse
    complement = col_hit.T - g_rows
    factor = jnp.dot(scaled, complement, precision=highest)
    carried_left = from_behind(left_b[-1], "row", 1)
    carried_right = from_behind(right_b[-1], "col", 1)
    updated = greens - jnp.dot(g_cols, factor, precision=highest)
    return whole_apply(updated, left_a, left_b, right_a, right_b, carried_left, carried_right)


def solution(mesh):
    return jax.shard_map(
        on_device,
        mesh=mesh,
        in_specs=(
            P("row", "col"),
            P(),
            P(),
            P("row", None, None),
            P("row", None, None),
            P("col", None, None),
            P("col", None, None),
        ),
        out_specs=P("row", "col"),
        check_vma=False,
    )
```

profile of v0, /device:TPU:0, one launch (start us, length us, event | category | flops | bytes accessed | tf_op | source)
XLA Modules:
  0.0 1041.7 jit_solution(11595491443462869906)
XLA Ops:
  6.6 3.4 fusion.4
  9.9 0.0 all-reduce.5.cloned.1.call-update
  10.0 0.0 all-reduce.7.cloned.1.call-start
  10.1 0.0 copy-start.9
  10.1 2.1 convolution_bitcast_fusion
  12.2 190.4 %all-reduce.5.cloned.1.call-done = f32[256,432]{0,1:T(8,128)} async-done(((f32[256,432]{0,1:T(8,128)}), f32[256,432]{0,1:T(8,128)}) %all-reduce.5.cloned.1.call-update) | async-done | bytes 442384 | tf_op jit(solution)/shard_map/psum | solution.py:84
  202.5 2.4 fusion.10
  204.9 0.0 all-reduce.7.cloned.1.call-update
  205.0 634.1 %all-reduce.7.cloned.1.call-done = (f32[864,256]{0,1:T(8,128)}, f32[256,256]{1,0:T(8,128)}) async-done(((f32[864,256]{0,1:T(8,128)}, f32[256,256]{1,0:T(8,128)}), (f32[864,256]{0,1:T(8,128)}, f32[256,256]{1,0:T(8,128)})) %all-reduce.7.cloned.1.call-update) | async-done | bytes 1146896 | tf_op jit(solution)/shard_map/psum | solution.py:83
  839.2 1.6 fusion.30
  840.8 1.7 fusion.29
  842.5 0.1 copy.16
  842.7 0.0 copy-start.5
  842.7 0.7 copy-done.5
  843.4 11.7 %cholesky.50 = f32[128,128]{1,0:T(8,128)S(1)} custom-call(f32[128,128]{1,0:T(8,128)S(1)} %cholesky.118), custom_call_target="Cholesky" | custom-call | tf_op jit(solution)/shard_map/jit(cholesky)/cholesky | solution.py:90
  855.1 9.8 custom-call.16
  865.0 1.0 constant_dynamic-update-slice_fusion.1
  866.0 1.1 convolution_subtract_fusion.3
  867.1 11.9 %cholesky.105 = f32[128,128]{1,0:T(8,128)S(1)} custom-call(f32[128,128]{1,0:T(8,128)S(1)} %convolution_subtract_fusion.3), custom_call_target="Cholesky" | custom-call | tf_op jit(solution)/shard_map/jit(cholesky)/cholesky | solution.py:90
  879.0 0.7 compare_reduce_fusion
  881.1 0.1 triangular_solve.71
  881.1 4.0 while.1
  881.1 0.6 fusion.70
  881.8 1.4 bitcast_dynamic-update-slice_fusion.2
  883.1 0.6 fusion.70
  883.8 1.4 bitcast_dynamic-update-slice_fusion.2
  885.1 19.7 %custom-call.17 = f32[2,128,128]{1,2,0:T(8,128)S(1)} custom-call(f32[2,128,128]{2,1,0:T(8,128)S(1)} %get-tuple-element.12), custom_call_target="InvertDiagBlocksLowerTriangular" | custom-call | tf_op jit(solution)/shard_map/triangular_solve | solution.py:92
  904.8 1.3 fusion.31
  906.1 1.3 convolution_subtract_fusion.2
  907.4 0.3 fusion.40
  907.7 0.3 fusion.39
  908.0 0.3 convolution_subtract_fusion.1
  908.3 0.3 fusion.38
  908.6 0.7 fusion.15
  909.3 2.8 convolution_subtract_fusion
  912.1 2.1 copy.17
  914.2 0.0 copy-start.3
  914.2 1.7 fusion.49
  916.0 1.9 collective-permute-start.2
  917.9 10.2 collective-permute-start.3
  928.2 0.0 copy-done.3
  928.2 2.1 collective-permute-start.1
  930.3 0.0 collective-permute-done.2
  930.3 0.5 collective-permute-done.3
  930.8 0.2 pad_maximum_fusion
  931.0 10.2 collective-permute-done.1
  941.3 1.9 fusion
  943.2 0.1 slice.98
  943.3 0.0 copy-start.6
  943.4 1.7 copy.18
  945.1 0.0 copy-done.6
  945.1 3.1 fusion.50
  948.2 0.8 fusion.48
  949.0 14.2 %collective-permute-start.4 = (f32[864,72]{0,1:T(8,128)}, f32[864,72]{0,1:T(8,128)}, u32[]{:S(2)}, u32[]{:S(2)}) collective-permute-start(f32[864,72]{0,1:T(8,128)} %get-tuple-element.27), channel_id=1, source_target_pairs={{0,1},{1,2},{2,3},{3,4},{4,5},{5,6},{6,7},{7,8},{8,9},{9,10},{10,1... | collective-permute-start | bytes 746504 | tf_op jit(solution)/shard_map/ppermute | solution.py:17
  963.2 48.1 %collective-permute-start.5 = (f32[864,72]{0,1:T(8,128)}, f32[864,72]{0,1:T(8,128)}, u32[]{:S(2)}, u32[]{:S(2)}) collective-permute-start(f32[864,72]{0,1:T(8,128)} %get-tuple-element.28), channel_id=1, source_target_pairs={{1,0},{2,1},{3,2},{4,3},{5,4},{6,5},{7,6},{8,7},{9,8},{10,9},{11,1... | collective-permute-start | bytes 746504 | tf_op jit(solution)/shard_map/ppermute | solution.py:18
  1011.3 0.0 copy-done.7
  1011.3 0.2 copy.14
  1011.6 1.9 collective-permute-start
  1013.5 0.5 collective-permute-done.4
  1014.0 1.5 collective-permute-done.5
  1015.4 1.2 pad_maximum_fusion.1
  1016.7 14.9 %collective-permute-done = f32[144,144]{0,1:T(8,128)S(1)} collective-permute-done((f32[144,144]{0,1:T(8,128)S(1)}, f32[144,144]{0,1:T(8,128)S(1)}, u32[]{:S(2)}, u32[]{:S(2)}) %collective-permute-start) | collective-permute-done | bytes 82976 | tf_op jit(solution)/shard_map/ppermute | solution.py:26
  1031.5 2.1 fusion.6
  1033.7 1.2 slice.101
  (29 shorter events, 0.3 us)
Async XLA Ops:
  6.5 907.6 %copy-start = (f32[6,144,144]{2,1,0:T(8,128)S(1)}, f32[6,144,144]{2,1,0:T(8,128)}, u32[]{:S(2)}) copy-start(f32[6,144,144]{2,1,0:T(8,128)} %param.10) | copy-start | bytes 1492996
  6.5 3.5 copy-start.1
  6.5 3.5 copy-start.8
  6.5 196.0 %all-reduce.5.cloned.1.call-start = ((), (), s32[]{:S(2)}) async-start(), calls=%async_computation | async-start | bytes 884736 | tf_op jit(solution)/shard_map/psum | solution.py:84
  10.0 829.2 %all-reduce.7.cloned.1.call-start = ((), (), s32[]{:S(2)}) async-start(), calls=%async_computation.1 | async-start | bytes 2359296 | tf_op jit(solution)/shard_map/psum | solution.py:83
  10.1 194.9 %copy-start.9 = (s32[256]{0:T(256)S(1)}, s32[256]{0:T(256)}, u32[]{:S(2)}) copy-start(s32[256]{0:T(256)} %param.9) | copy-start | bytes 3076
  842.7 0.7 copy-start.5
  881.0 27.6 %copy-start.2 = (f32[256,432]{0,1:T(8,128)S(1)}, f32[256,432]{0,1:T(8,128)}, u32[]{:S(2)}) copy-start(f32[256,432]{0,1:T(8,128)} %all-reduce.5.cloned.1.call-done) | copy-start | bytes 1327108
  904.8 4.5 copy-start.4
  914.2 14.0 %copy-start.3 = (f32[6,144,144]{2,1,0:T(8,128)S(1)}, f32[6,144,144]{2,1,0:T(8,128)}, u32[]{:S(2)}) copy-start(f32[6,144,144]{2,1,0:T(8,128)} %param.11) | copy-start | bytes 1492996
  916.0 14.4 %collective-permute-start.2 = (f32[72,432]{1,0:T(8,128)S(1)}, f32[72,432]{1,0:T(8,128)S(1)}, u32[]{:S(2)}, u32[]{:S(2)}) collective-permute-start(f32[72,432]{1,0:T(8,128)S(1)} %get-tuple-element.25), channel_id=1, source_target_pairs={{0,32},{32,64},{64,96},{96,128},{128,160},{160,192},{192,224},{224... | collective-permute-start | bytes 373256 | tf_op jit(solution)/shard_map/ppermute | solution.py:17
  917.9 12.9 %collective-permute-start.3 = (f32[72,432]{1,0:T(8,128)S(1)}, f32[72,432]{1,0:T(8,128)S(1)}, u32[]{:S(2)}, u32[]{:S(2)}) collective-permute-start(f32[72,432]{1,0:T(8,128)S(1)} %get-tuple-element.26), channel_id=1, source_target_pairs={{32,0},{64,32},{96,64},{128,96},{160,128},{192,160},{224,192},{256... | collective-permute-start | bytes 373256 | tf_op jit(solution)/shard_map/ppermute | solution.py:18
  928.2 13.1 %collective-permute-start.1 = (f32[144,144]{1,0:T(8,128)S(1)}, f32[144,144]{1,0:T(8,128)S(1)}, u32[]{:S(2)}, u32[]{:S(2)}) collective-permute-start(f32[144,144]{1,0:T(8,128)S(1)} %slice_bitcast_fusion.1), channel_id=1, source_target_pairs={{0,32},{32,64},{64,96},{96,128},{128,160},{160,192},{192,224},{224... | collective-permute-start | bytes 248840 | tf_op jit(solution)/shard_map/ppermute | solution.py:26
  943.3 1.7 copy-start.6
  945.1 66.3 %copy-start.7 = (f32[3,144,144]{2,1,0:T(8,128)S(1)}, f32[3,144,144]{2,1,0:T(8,128)}, u32[]{:S(2)}) copy-start(f32[3,144,144]{2,1,0:T(8,128)} %param.13) | copy-start | bytes 746500
  949.0 65.0 %collective-permute-start.4 = (f32[864,72]{0,1:T(8,128)}, f32[864,72]{0,1:T(8,128)}, u32[]{:S(2)}, u32[]{:S(2)}) collective-permute-start(f32[864,72]{0,1:T(8,128)} %get-tuple-element.27), channel_id=1, source_target_pairs={{0,1},{1,2},{2,3},{3,4},{4,5},{5,6},{6,7},{7,8},{8,9},{9,10},{10,1... | collective-permute-start | bytes 746504 | tf_op jit(solution)/shard_map/ppermute | solution.py:17
  963.2 52.2 %collective-permute-start.5 = (f32[864,72]{0,1:T(8,128)}, f32[864,72]{0,1:T(8,128)}, u32[]{:S(2)}, u32[]{:S(2)}) collective-permute-start(f32[864,72]{0,1:T(8,128)} %get-tuple-element.28), channel_id=1, source_target_pairs={{1,0},{2,1},{3,2},{4,3},{5,4},{6,5},{7,6},{8,7},{9,8},{10,9},{11,1... | collective-permute-start | bytes 746504 | tf_op jit(solution)/shard_map/ppermute | solution.py:18
  1011.6 20.0 %collective-permute-start = (f32[144,144]{0,1:T(8,128)S(1)}, f32[144,144]{0,1:T(8,128)S(1)}, u32[]{:S(2)}, u32[]{:S(2)}) collective-permute-start(f32[144,144]{0,1:T(8,128)S(1)} %slice_bitcast_fusion), channel_id=1, source_target_pairs={{0,1},{1,2},{2,3},{3,4},{4,5},{5,6},{6,7},{7,8},{8,9},{9,10},{10,1... | collective-permute-start | bytes 248840 | tf_op jit(solution)/shard_map/ppermute | solution.py:26
Sparse Core Ops, SparseCore 0:
  10.3 192.2 all-reduce.4
  205.8 633.3 all-reduce.6
where the time goes:
time: 1040 us
  waiting for transfers between devices  852 us (82%)
  starting transfers between devices  78.5 us (8%)
  other arithmetic  57 us (5%)
  matrix products  27.8 us (3%)
  between operations  15.1 us (1%)
  local copies, waits for them, and re-layouts  11.1 us (1%)
    psum x1, waiting for transfers between devices, on_device(): g_cols = lax.psum(jnp.dot(greens, col_hit, precision=highest), 'col')  634 us
    psum x1, waiting for transfers between devices, on_device(): g_rows = lax.psum(jnp.dot(row_hit, greens, precision=highest), 'row')  190 us
    ppermute x2, starting transfers between devices, padded_2(): after = lax.ppermute(leading, axis, down)  58.3 us
    another operation x6, other arithmetic, on_device(): lower_factor = jnp.linalg.cholesky(normal_matrix)  34.2 us
    ppermute x2, waiting for transfers between devices, from_behind(): return lax.ppermute(value, axis, pairs)  25.1 us
  transfers between devices with their start and end apart: 8, of which 7 were waited for; matrix products, arithmetic and copies ran while one was open for 0% of the time, Pallas kernels for 0%

commit v1 on v0

--- a/solution.py
+++ b/solution.py
@@ -81,7 +81,9 @@
         accepted_sites[:, None] == row_base + lax.broadcasted_iota(jnp.int32, (accepted, height), 1)
     ).astype(jnp.float32)
     g_cols = lax.psum(jnp.dot(greens, col_hit, precision=highest), "col")
-    g_rows = lax.psum(jnp.dot(row_hit, greens, precision=highest), "row")
+    own = jnp.dot(row_hit, greens, precision=highest)
+    parts = lax.all_gather(own, "row", axis=0, tiled=False)
+    g_rows = parts.sum(axis=0)
     g_pair = lax.psum(jnp.dot(g_rows, col_hit, precision=highest), "col")
     shifts = jnp.exp(-2.0 * coupling * field_values.astype(jnp.float32)) - 1.0
     identity = jnp.eye(accepted, dtype=jnp.float32)

time: 1040 us -> 966 us (0.929)
  waiting for transfers between devices: 852 us -> 767 us
    psum x1 -> x0, waiting for transfers between devices: 190 us -> none  [on_device(): g_rows = lax.psum(jnp.dot(row_hit, greens, precision=highest), 'row')]
    all_gather x0 -> x1, waiting for transfers between devices: none -> 111 us  [on_device(): parts = lax.all_gather(own, 'row', axis=0, tiled=False)]
    ppermute x2, starting transfers between devices: 58.3 us -> 22.1 us  [padded_2(): after = lax.ppermute(leading, axis, down)]
    ppermute x2, starting transfers between devices: 16.1 us -> 49.7 us  [padded_2(): before = lax.ppermute(last, axis, up)]
  transfers between devices with their start and end apart: 8 -> 8, of which waited for: 7 -> 6; matrix products, arithmetic and copies ran while one was open for 0% -> 0% of each run, Pallas kernels for 0% -> 0%
where the time goes in v1:
time: 966 us; the launch traced here: 963 us
  waiting for transfers between devices  767 us (79%)
  starting transfers between devices  76.5 us (8%)
  other arithmetic  59.7 us (6%)
  matrix products  27.2 us (3%)
  local copies, waits for them, and re-layouts  17.7 us (2%)
  between operations  15 us (2%)
    psum x1, waiting for transfers between devices, on_device(): g_cols = lax.psum(jnp.dot(greens, col_hit, precision=highest), 'col')  629 us
    all_gather x1, waiting for transfers between devices, on_device(): parts = lax.all_gather(own, 'row', axis=0, tiled=False)  111 us
    ppermute x2, starting transfers between devices, padded_2(): before = lax.ppermute(last, axis, up)  49.7 us
    another operation x6, other arithmetic, on_device(): lower_factor = jnp.linalg.cholesky(normal_matrix)  34.2 us
    ppermute x2, waiting for transfers between devices, from_behind(): return lax.ppermute(value, axis, pairs)  24 us
    ppermute x2, starting transfers between devices, padded_2(): after = lax.ppermute(leading, axis, down)  22.1 us
    another operation x3, other arithmetic, on_device(): lax.linalg.triangular_solve(lower_factor, middle, left_side=True, lower=T...  19.7 us
  transfers between devices with their start and end apart: 8, of which 6 were waited for; matrix products, arithmetic and copies ran while one was open for 0% of the time, Pallas kernels for 0%

profile of v1, /device:TPU:0, one launch (start us, length us, event | category | flops | bytes accessed | tf_op | source)
XLA Modules:
  0.0 963.1 jit_solution(754197896855138678)
XLA Ops:
  6.6 3.4 fusion.4
  9.9 0.0 all-gather.3.cloned.1.call-update
  10.0 0.0 all-reduce.4.cloned.1.call-start
  10.0 0.0 copy-done.1
  10.1 2.6 convolution_bitcast_fusion
  12.6 110.9 %all-gather.3.cloned.1.call-done = f32[4096,432]{0,1:T(8,128)} async-done(((f32[256,432]{0,1:T(8,128)}), f32[4096,432]{0,1:T(8,128)}) %all-gather.3.cloned.1.call-update) | async-done | bytes 7077904 | tf_op jit(solution)/shard_map/all_gather | solution.py:85
  123.6 6.2 copy.29
  129.8 1.9 bitcast_reduce_fusion
  131.7 0.0 copy-start.7
  131.7 1.4 fusion.10
  133.1 0.0 all-reduce.4.cloned.1.call-update
  133.2 629.0 %all-reduce.4.cloned.1.call-done = (f32[864,256]{1,0:T(8,128)}, f32[256,256]{1,0:T(8,128)}) async-done(((f32[864,256]{1,0:T(8,128)}, f32[256,256]{1,0:T(8,128)}), (f32[864,256]{1,0:T(8,128)}, f32[256,256]{1,0:T(8,128)})) %all-reduce.4.cloned.1.call-update) | async-done | bytes 1146896 | tf_op jit(solution)/shard_map/psum | solution.py:83
  762.2 1.6 fusion.30
  763.8 1.7 fusion.29
  765.5 0.1 copy.22
  765.6 0.7 fusion.22
  766.4 0.8 cholesky.118
  767.2 11.7 %cholesky.50 = f32[128,128]{1,0:T(8,128)S(1)} custom-call(f32[128,128]{1,0:T(8,128)S(1)} %cholesky.118), custom_call_target="Cholesky" | custom-call | tf_op jit(solution)/shard_map/jit(cholesky)/cholesky | solution.py:92
  779.0 9.8 %custom-call.16 = f32[1,128,128]{1,2,0:T(8,128)S(1)} custom-call(f32[1,128,128]{2,1,0:T(8,128)S(1)} %get-tuple-element.32), custom_call_target="InvertDiagBlocksLowerTriangular" | custom-call | tf_op jit(solution)/shard_map/jit(cholesky)/cholesky | solution.py:92
  788.8 1.0 constant_dynamic-update-slice_fusion.1
  789.9 1.1 convolution_subtract_fusion.3
  791.0 11.9 %cholesky.105 = f32[128,128]{1,0:T(8,128)S(1)} custom-call(f32[128,128]{1,0:T(8,128)S(1)} %convolution_subtract_fusion.3), custom_call_target="Cholesky" | custom-call | tf_op jit(solution)/shard_map/jit(cholesky)/cholesky | solution.py:92
  802.9 0.7 compare_reduce_fusion
  804.9 0.1 triangular_solve.71
  804.9 3.9 while.1
  804.9 0.6 fusion.70
  805.6 1.3 bitcast_dynamic-update-slice_fusion.2
  806.9 0.6 fusion.70
  807.6 1.3 bitcast_dynamic-update-slice_fusion.2
  808.9 19.7 %custom-call.17 = f32[2,128,128]{1,2,0:T(8,128)S(1)} custom-call(f32[2,128,128]{2,1,0:T(8,128)S(1)} %get-tuple-element.12), custom_call_target="InvertDiagBlocksLowerTriangular" | custom-call | tf_op jit(solution)/shard_map/triangular_solve | solution.py:94
  828.6 1.3 fusion.31
  829.9 1.3 convolution_subtract_fusion.2
  831.2 0.3 fusion.40
  831.5 0.3 fusion.39
  831.8 0.3 convolution_subtract_fusion.1
  832.1 0.3 fusion.38
  832.3 0.6 fusion.15
  833.0 2.7 convolution_subtract_fusion
  835.7 2.1 copy.24
  837.8 0.0 copy-start.2
  837.8 1.7 fusion.49
  839.6 1.9 collective-permute-start.2
  841.5 10.2 %collective-permute-start.3 = (f32[72,432]{1,0:T(8,128)S(1)}, f32[72,432]{1,0:T(8,128)S(1)}, u32[]{:S(2)}, u32[]{:S(2)}) collective-permute-start(f32[72,432]{1,0:T(8,128)S(1)} %get-tuple-element.26), channel_id=1, source_target_pairs={{32,0},{64,32},{96,64},{128,96},{160,128},{192,160},{224,192},{256... | collective-permute-start | bytes 373256 | tf_op jit(solution)/shard_map/ppermute | solution.py:18
  851.8 1.9 collective-permute-start.1
  853.7 0.0 collective-permute-done.2
  853.7 0.7 collective-permute-done.3
  854.4 0.2 pad_maximum_fusion
  854.6 10.3 %collective-permute-done.1 = f32[144,144]{1,0:T(8,128)S(1)} collective-permute-done((f32[144,144]{1,0:T(8,128)S(1)}, f32[144,144]{1,0:T(8,128)S(1)}, u32[]{:S(2)}, u32[]{:S(2)}) %collective-permute-start.1) | collective-permute-done | bytes 82976 | tf_op jit(solution)/shard_map/ppermute | solution.py:26
  864.9 1.9 fusion
  866.8 0.1 slice.98
  867.0 0.0 copy-start.4
  867.0 2.0 copy.25
  869.0 3.1 fusion.50
  872.1 0.8 fusion.48
  872.9 47.8 %collective-permute-start.4 = (f32[864,72]{0,1:T(8,128)}, f32[864,72]{0,1:T(8,128)}, u32[]{:S(2)}, u32[]{:S(2)}) collective-permute-start(f32[864,72]{0,1:T(8,128)} %get-tuple-element.27), channel_id=1, source_target_pairs={{0,1},{1,2},{2,3},{3,4},{4,5},{5,6},{6,7},{7,8},{8,9},{9,10},{10,1... | collective-permute-start | bytes 746504 | tf_op jit(solution)/shard_map/ppermute | solution.py:17
  920.8 11.9 %collective-permute-start.5 = (f32[864,72]{0,1:T(8,128)}, f32[864,72]{0,1:T(8,128)}, u32[]{:S(2)}, u32[]{:S(2)}) collective-permute-start(f32[864,72]{0,1:T(8,128)} %get-tuple-element.28), channel_id=1, source_target_pairs={{1,0},{2,1},{3,2},{4,3},{5,4},{6,5},{7,6},{8,7},{9,8},{10,9},{11,1... | collective-permute-start | bytes 746504 | tf_op jit(solution)/shard_map/ppermute | solution.py:18
  932.7 0.2 copy.20
  932.9 2.7 collective-permute-start
  935.6 0.0 collective-permute-done.4
  935.6 2.4 collective-permute-done.5
  938.0 1.2 pad_maximum_fusion.1
  939.2 13.7 %collective-permute-done = f32[144,144]{0,1:T(8,128)S(1)} collective-permute-done((f32[144,144]{0,1:T(8,128)S(1)}, f32[144,144]{0,1:T(8,128)S(1)}, u32[]{:S(2)}, u32[]{:S(2)}) %collective-permute-start) | collective-permute-done | bytes 82976 | tf_op jit(solution)/shard_map/ppermute | solution.py:26
  952.9 2.1 fusion.6
  955.0 1.2 slice.101
  (27 shorter events, 0.2 us)
Async XLA Ops:
  6.5 831.3 %copy-start = (f32[6,144,144]{2,1,0:T(8,128)S(1)}, f32[6,144,144]{2,1,0:T(8,128)}, u32[]{:S(2)}) copy-start(f32[6,144,144]{2,1,0:T(8,128)} %param.10) | copy-start | bytes 1492996
  6.5 3.5 copy-start.1
  6.5 3.5 copy-start.6
  6.5 117.0 %all-gather.3.cloned.1.call-start = ((), (), s32[]{:S(2)}) async-start(), calls=%async_computation | async-start | bytes 7520256 | tf_op jit(solution)/shard_map/all_gather | solution.py:85
  10.0 752.2 %all-reduce.4.cloned.1.call-start = ((), (), s32[]{:S(2)}) async-start(), calls=%async_computation.1 | async-start | bytes 2293760 | tf_op jit(solution)/shard_map/psum | solution.py:83
  131.7 1.5 copy-start.7
  828.6 4.4 copy-start.3
  837.8 14.0 %copy-start.2 = (f32[6,144,144]{2,1,0:T(8,128)S(1)}, f32[6,144,144]{2,1,0:T(8,128)}, u32[]{:S(2)}) copy-start(f32[6,144,144]{2,1,0:T(8,128)} %param.11) | copy-start | bytes 1492996
  839.6 14.1 %collective-permute-start.2 = (f32[72,432]{1,0:T(8,128)S(1)}, f32[72,432]{1,0:T(8,128)S(1)}, u32[]{:S(2)}, u32[]{:S(2)}) collective-permute-start(f32[72,432]{1,0:T(8,128)S(1)} %get-tuple-element.25), channel_id=1, source_target_pairs={{0,32},{32,64},{64,96},{96,128},{128,160},{160,192},{192,224},{224... | collective-permute-start | bytes 373256 | tf_op jit(solution)/shard_map/ppermute | solution.py:17
  841.5 12.9 %collective-permute-start.3 = (f32[72,432]{1,0:T(8,128)S(1)}, f32[72,432]{1,0:T(8,128)S(1)}, u32[]{:S(2)}, u32[]{:S(2)}) collective-permute-start(f32[72,432]{1,0:T(8,128)S(1)} %get-tuple-element.26), channel_id=1, source_target_pairs={{32,0},{64,32},{96,64},{128,96},{160,128},{192,160},{224,192},{256... | collective-permute-start | bytes 373256 | tf_op jit(solution)/shard_map/ppermute | solution.py:18
  851.8 13.1 %collective-permute-start.1 = (f32[144,144]{1,0:T(8,128)S(1)}, f32[144,144]{1,0:T(8,128)S(1)}, u32[]{:S(2)}, u32[]{:S(2)}) collective-permute-start(f32[144,144]{1,0:T(8,128)S(1)} %slice_bitcast_fusion.1), channel_id=1, source_target_pairs={{0,32},{32,64},{64,96},{96,128},{128,160},{160,192},{192,224},{224... | collective-permute-start | bytes 248840 | tf_op jit(solution)/shard_map/ppermute | solution.py:26
  867.0 2.0 copy-start.4
  869.0 63.7 %copy-start.5 = (f32[3,144,144]{2,1,0:T(8,128)S(1)}, f32[3,144,144]{2,1,0:T(8,128)}, u32[]{:S(2)}) copy-start(f32[3,144,144]{2,1,0:T(8,128)} %param.13) | copy-start | bytes 746500
  872.9 62.7 %collective-permute-start.4 = (f32[864,72]{0,1:T(8,128)}, f32[864,72]{0,1:T(8,128)}, u32[]{:S(2)}, u32[]{:S(2)}) collective-permute-start(f32[864,72]{0,1:T(8,128)} %get-tuple-element.27), channel_id=1, source_target_pairs={{0,1},{1,2},{2,3},{3,4},{4,5},{5,6},{6,7},{7,8},{8,9},{9,10},{10,1... | collective-permute-start | bytes 746504 | tf_op jit(solution)/shard_map/ppermute | solution.py:17
  920.8 17.3 %collective-permute-start.5 = (f32[864,72]{0,1:T(8,128)}, f32[864,72]{0,1:T(8,128)}, u32[]{:S(2)}, u32[]{:S(2)}) collective-permute-start(f32[864,72]{0,1:T(8,128)} %get-tuple-element.28), channel_id=1, source_target_pairs={{1,0},{2,1},{3,2},{4,3},{5,4},{6,5},{7,6},{8,7},{9,8},{10,9},{11,1... | collective-permute-start | bytes 746504 | tf_op jit(solution)/shard_map/ppermute | solution.py:18
  932.9 20.0 %collective-permute-start = (f32[144,144]{0,1:T(8,128)S(1)}, f32[144,144]{0,1:T(8,128)S(1)}, u32[]{:S(2)}, u32[]{:S(2)}) collective-permute-start(f32[144,144]{0,1:T(8,128)S(1)} %slice_bitcast_fusion), channel_id=1, source_target_pairs={{0,1},{1,2},{2,3},{3,4},{4,5},{5,6},{6,7},{7,8},{8,9},{9,10},{10,1... | collective-permute-start | bytes 248840 | tf_op jit(solution)/shard_map/ppermute | solution.py:26
Sparse Core Ops, SparseCore 0:
  10.1 113.4 all-gather.2
  133.3 628.8 all-reduce.3
